TPU v7x, 256 devices: a whole 4x4x8 slice. The times are simulated.
256 devices in a mesh: row: 8 (over y, core), col: 32 (over z, x).
Axes of the slice: x: 4, y: 4, z: 8, core: 2. Of those that a mesh axis runs over, the one named last changes fastest.
Arguments:
- source: bfloat16 [16384, 512], P('row'), may hold values from -16 to 16
- target: bfloat16 [16384, 512], P('col'), may hold values from -6 to 6
- log_source_mass: float32 [16384], P('row'), may hold values from -1.5 to 1.5
- log_target_mass: float32 [16384], P('col'), may hold values from -1.5 to 1.5
Outputs:
- source_image: float32 [16384, 512], P(('row', 'col'))
- target_image: float32 [16384, 512], P('col')
All inputs are finite; a program needn't handle non-finite values.
Results may differ from a plain program's by a relative error of at most 0.0055.
Values sent between devices are 32-bit elements; how exact they have to be, the bound alone decides.
A program may use at most 64 MiB of HBM per device.

v0:
```python
import jax
import jax.numpy as jnp
from jax import lax
from jax.sharding import PartitionSpec as P

D = 512
ITERS = 2


blur = 0.1


def tile_cost(source, target, sqx, sqy):
    inner = jnp.dot(source, target.T, preferred_element_type=jnp.float32)
    return (sqx[:, None] + sqy[None, :] - 2.0 * inner) / D


def across_targets(scores):
    local_peak = jnp.max(scores, axis=1)
    peak = lax.pmax(local_peak, "col")
    total = lax.psum(jnp.sum(jnp.exp(scores - peak[:, None]), axis=1), "col")
    return peak + jnp.log(total)


def across_sources(scores):
    local_peak = jnp.max(scores, axis=0)
    peak = lax.pmax(local_peak, "row")
    total = lax.psum(jnp.sum(jnp.exp(scores - peak[None, :]), axis=0), "row")
    return peak + jnp.log(total)


def on_device(source, target, log_source_mass, log_target_mass):
    sqx = jnp.einsum("id,id->i", source, source, preferred_element_type=jnp.float32)
    sqy = jnp.einsum("id,id->i", target, target, preferred_element_type=jnp.float32)
    g_pot = jnp.zeros((target.shape[0],), jnp.float32)
    f_pot = jnp.zeros((source.shape[0],), jnp.float32)
    for step in range(ITERS):
        cost = tile_cost(source, target, sqx, sqy)
        f_pot = -blur * across_targets(log_target_mass[None, :] + (g_pot[None, :] - cost) / blur)
        cost = tile_cost(source, target, sqx, sqy)
        g_pot = -blur * across_sources(log_source_mass[:, None] + (f_pot[:, None] - cost) / blur)
    cost = tile_cost(source, target, sqx, sqy)
    plan = jnp.exp(
        log_source_mass[:, None]
        + log_target_mass[None, :]
        + (f_pot[:, None] + g_pot[None, :] - cost) / blur
    )
    weights = plan.astype(jnp.bfloat16)
    src_numer = jnp.dot(weights, target, preferred_element_type=jnp.float32)
    src_denom = jnp.sum(plan, axis=1)
    tgt_numer = lax.dot_general(
        weights, source, (((0,), (0,)), ((), ())), preferred_element_type=jnp.float32
    )
    tgt_denom = jnp.sum(plan, axis=0)
    full_numer, full_denom = lax.psum((src_numer, src_denom), "col")
    count = source.shape[0] // lax.axis_size("col")
    start = lax.axis_index("col") * count
    own_numer = lax.dynamic_slice_in_dim(full_numer, start, count, 0)
    own_denom = lax.dynamic_slice_in_dim(full_denom, start, count, 0)
    source_image = own_numer / own_denom[:, None]
    all_numer, all_denom = lax.psum((tgt_numer, tgt_denom), "row")
    target_image = all_numer / all_denom[:, None]
    return (source_image, target_image)


def solution(mesh):
    in_specs = (P("row", None), P("col", None), P("row"), P("col"))
    out_specs = (P(("row", "col"), None), P("col", None))
    return jax.shard_map(
        on_device, mesh=mesh, in_specs=in_specs, out_specs=out_specs, check_vma=False
    )
```

profile of v0, /device:TPU:1, one launch (start us, length us, event | category | flops | bytes accessed | tf_op | source)
XLA Modules:
  0.0 619.9 jit_solution(15037420274300884505)
XLA Ops:
  7.2 0.0 all-reduce.5.cloned.1.call-start
  7.2 2.1 fusion
  9.3 1.2 fusion.5
  10.5 0.0 copy-start.3
  10.5 5.6 fusion.1
  16.2 0.0 copy-start.2
  16.2 65.3 %pmax.28 = f32[2048]{0:T(1024)S(1)} all-reduce(f32[2048]{0:T(1024)S(1)} %get-tuple-element.4), channel_id=1, replica_groups=mesh['row'=8,'col'=32] {'col'}, use_global_device_ids=true, to_apply=%region_1.0 | all-reduce | flops 2048 | bytes 16384 | tf_op jit(solution)/shard_map/pmax | solution.py:20
  81.5 0.0 copy-done.3
  81.5 3.4 exponential_reduce_fusion.3
  84.9 56.8 %psum.56 = f32[2048]{0:T(1024)S(1)} all-reduce(f32[2048]{0:T(1024)S(1)} %exponential_reduce_fusion.3), channel_id=1, replica_groups=mesh['row'=8,'col'=32] {'col'}, use_global_device_ids=true, to_apply=%region_3.0 | all-reduce | flops 2048 | bytes 16384 | tf_op jit(solution)/shard_map/psum | solution.py:21
  141.7 0.0 copy-done.2
  141.7 2.6 fusion.2
  144.3 40.6 %pmax.29 = f32[512]{0:T(512)S(1)} all-reduce(f32[512]{0:T(512)S(1)} %fusion.2), channel_id=1, replica_groups=mesh['row'=8,'col'=32] {'row'}, use_global_device_ids=true, to_apply=%region_5.0 | all-reduce | flops 512 | bytes 4096 | tf_op jit(solution)/shard_map/pmax | solution.py:27
  185.0 2.8 exponential_reduce_fusion.2
  187.8 12.2 %psum.57 = f32[512]{0:T(512)S(1)} all-reduce(f32[512]{0:T(512)S(1)} %exponential_reduce_fusion.2), channel_id=1, replica_groups=mesh['row'=8,'col'=32] {'row'}, use_global_device_ids=true, to_apply=%region_7.0 | all-reduce | flops 512 | bytes 4096 | tf_op jit(solution)/shard_map/psum | solution.py:28
  200.0 2.8 fusion.3
  202.8 58.5 %pmax.30 = f32[2048]{0:T(1024)S(1)} all-reduce(f32[2048]{0:T(1024)S(1)} %fusion.3), channel_id=1, replica_groups=mesh['row'=8,'col'=32] {'col'}, use_global_device_ids=true, to_apply=%region_9.0 | all-reduce | flops 2048 | bytes 16384 | tf_op jit(solution)/shard_map/pmax | solution.py:20
  261.3 3.4 exponential_reduce_fusion.1
  264.7 56.8 %psum.58 = f32[2048]{0:T(1024)S(1)} all-reduce(f32[2048]{0:T(1024)S(1)} %exponential_reduce_fusion.1), channel_id=1, replica_groups=mesh['row'=8,'col'=32] {'col'}, use_global_device_ids=true, to_apply=%region_11.0 | all-reduce | flops 2048 | bytes 16384 | tf_op jit(solution)/shard_map/psum | solution.py:21
  321.5 0.0 copy-start
  321.6 2.7 fusion.4
  324.3 40.5 %pmax.31 = f32[512]{0:T(512)S(1)} all-reduce(f32[512]{0:T(512)S(1)} %fusion.4), channel_id=1, replica_groups=mesh['row'=8,'col'=32] {'row'}, use_global_device_ids=true, to_apply=%region_13.0 | all-reduce | flops 512 | bytes 4096 | tf_op jit(solution)/shard_map/pmax | solution.py:27
  364.8 2.8 exponential_reduce_fusion
  367.6 12.4 %psum.59 = f32[512]{0:T(512)S(1)} all-reduce(f32[512]{0:T(512)S(1)} %exponential_reduce_fusion), channel_id=1, replica_groups=mesh['row'=8,'col'=32] {'row'}, use_global_device_ids=true, to_apply=%region_15.0 | all-reduce | flops 512 | bytes 4096 | tf_op jit(solution)/shard_map/psum | solution.py:28
  380.0 0.0 copy-done
  380.0 0.0 copy-start.1
  380.0 5.6 fusion.6
  385.6 0.0 all-reduce.5.cloned.1.call-update
  385.6 0.2 all-reduce.3.cloned.1.call-start
  385.8 0.0 copy-done.1
  385.8 5.8 fusion.8
  391.6 0.0 all-reduce.3.cloned.1.call-update
  391.7 3.2 fusion.10
  394.9 59.2 %psum.61 = f32[2048]{0:T(1024)S(1)} all-reduce(f32[2048]{0:T(1024)S(1)} %get-tuple-element.3), channel_id=1, replica_groups=mesh['row'=8,'col'=32] {'col'}, use_global_device_ids=true, to_apply=%region_18.0 | all-reduce | flops 2048 | bytes 16384 | tf_op jit(solution)/shard_map/psum | solution.py:55
  454.0 0.1 dynamic_slice.7
  454.1 26.5 %psum.63 = f32[512]{0:T(512)S(1)} all-reduce(f32[512]{0:T(512)S(1)} %get-tuple-element.2), channel_id=1, replica_groups=mesh['row'=8,'col'=32] {'row'}, use_global_device_ids=true, to_apply=%region_21.0 | all-reduce | flops 512 | bytes 4096 | tf_op jit(solution)/shard_map/psum | solution.py:61
  480.6 0.0 all-reduce.5.cloned.1.call-done
  480.6 2.3 broadcast_divide_fusion
  482.9 128.5 %all-reduce.3.cloned.1.call-done = f32[2048,512]{1,0:T(8,128)} async-done(((f32[2048,512]{1,0:T(8,128)}), f32[2048,512]{1,0:T(8,128)}) %all-reduce.3.cloned.1.call-update) | async-done | bytes 4194320 | tf_op jit(solution)/shard_map/psum | solution.py:55
  611.4 1.6 dynamic-slice_divide_fusion
  (4 shorter events, 0.0 us)
Async XLA Ops:
  7.2 473.4 %all-reduce.5.cloned.1.call-start = ((), (), s32[]{:S(2)}) async-start(), calls=%async_computation.1 | async-start | bytes 2097152 | tf_op jit(solution)/shard_map/psum | solution.py:61
  10.5 71.0 %copy-start.3 = (f32[512]{0:T(512)S(1)}, f32[512]{0:T(512)}, u32[]{:S(2)}) copy-start(f32[512]{0:T(512)} %param.7) | copy-start | bytes 6148
  16.2 125.5 %copy-start.2 = (f32[2048]{0:T(1024)S(1)}, f32[2048]{0:T(1024)}, u32[]{:S(2)}) copy-start(f32[2048]{0:T(1024)} %param.6) | copy-start | bytes 24580
  321.5 58.4 %copy-start = (bf16[2048,512]{1,0:T(8,128)(2,1)S(1)}, bf16[2048,512]{1,0:T(8,128)(2,1)}, u32[]{:S(2)}) copy-start(bf16[2048,512]{1,0:T(8,128)(2,1)} %param.4) | copy-start | bytes 6291460
  380.0 5.8 copy-start.1
  385.6 225.8 %all-reduce.3.cloned.1.call-start = ((), (), s32[]{:S(2)}) async-start(), calls=%async_computation | async-start | bytes 8388608 | tf_op jit(solution)/shard_map/psum | solution.py:55
Sparse Core Ops, SparseCore 0:
  385.7 59.2 all-reduce.4
  448.6 162.7 all-reduce.2
where the time goes:
time: 622 us; the launch traced here: 620 us
  blocking collectives  429 us (69%)
  waiting for transfers between devices  128 us (21%)
  other arithmetic  30.9 us (5%)
  matrix products  17 us (3%)
  between operations  14.2 us (2%)
    psum x1, waiting for transfers between devices, on_device(): full_numer, full_denom = lax.psum((src_numer, src_denom), 'col')  128 us
    pmax x2, blocking collectives, across_targets(): peak = lax.pmax(local_peak, 'col')  124 us
    psum x2, blocking collectives, across_targets(): total = lax.psum(jnp.sum(jnp.exp(scores - peak[:, None]), axis=1), 'col')  114 us
    pmax x2, blocking collectives, across_sources(): peak = lax.pmax(local_peak, 'row')  81.1 us
    psum x1, blocking collectives, on_device(): full_numer, full_denom = lax.psum((src_numer, src_denom), 'col')  59.2 us
    psum x1, blocking collectives, on_device(): all_numer, all_denom = lax.psum((tgt_numer, tgt_denom), 'row')  26.5 us
    psum x2, blocking collectives, across_sources(): total = lax.psum(jnp.sum(jnp.exp(scores - peak[None, :]), axis=0), 'row')  24.7 us
  transfers between devices with their start and end apart: 2, of which 1 were waited for; matrix products, arithmetic and copies ran while one was open for 2% of the time, Pallas kernels for 0%

commit v1 on v0

v1 whole, which is shorter than its diff:
```python
import functools
import math

import jax
import jax.numpy as jnp
from jax import lax
from jax.experimental import pallas as pl
from jax.experimental.pallas import tpu as pltpu
from jax.sharding import PartitionSpec as P

D = 512
NI = 2048
NJ = 512
NY, NK, NZ, NX = 4, 2, 8, 4
OWN = NI // (NZ * NX)
HALF = NJ // NK
QUART = HALF // NY
BLUR = 0.1
LOG2E = math.log2(math.e)
NORM = LOG2E / (D * BLUR)
MESH = pl.DeviceIdType.MESH
F32 = jnp.float32
BF16 = jnp.bfloat16

X_PEERS = [1, 2, 3]
Y_PEERS = [2, 1, 3]
Z_PEERS = [4, 3, 5, 2, 6, 1, 7]
ROW_PEERS = [(dy, dk) for dy in (2, 1, 3, 0) for dk in (1, 0) if (dy, dk) != (0, 0)]
WIDE_PEERS = [
    (dy, dk, dx) for dy in (2, 1, 3, 0) for dx in (2, 1, 3, 0) for dk in (1, 0) if (dy, dk, dx) != (0, 0, 0)
]


def log2(x):
    return jnp.log(x) * LOG2E


def merge(parts):
    peak = functools.reduce(jnp.maximum, parts)
    return peak + log2(sum(jnp.exp2(part - peak) for part in parts))


def merge_rows(x):
    peak = jnp.max(x, axis=0, keepdims=True)
    return peak + log2(jnp.sum(jnp.exp2(x - peak), axis=0, keepdims=True))


def to_column(row):
    return jnp.broadcast_to(row, (128, row.shape[1])).T


def nt_dot(a, b):
    return lax.dot_general(a, b, (((1,), (1,)), ((), ())), preferred_element_type=F32)


def squared_norms(x):
    sq = x.astype(F32)
    sq = sq * sq
    high = sq.astype(BF16)
    low = (sq - high.astype(F32)).astype(BF16)
    ones = jnp.ones((8, D), BF16)
    return (nt_dot(ones, high) + nt_dot(ones, low))[:1]


def kernel(
    src, tgt, lsm, ltm, simg, timg,
    xt, x2, t4, tf, trecv, own, fparts, gparts, acol, browb, num, dparts,
    aux, auxr, lf, lfx, lfz, lg, lgr, lgw, bcol,
    tn, tsib, tc, ty, tout, plus, minus, dn, dnr,
    pf_s, pf_r, sib_s, sib_r, aux_s, aux_r, fx_s, fx_r, fz_s, fz_r, gr_s, gr_r, gw_s, gw_r,
    ts_s, ts_r, ty_s, ty_r, ta_s, ta_r, tb_s, tb_r, plus_s, plus_r, minus_s, minus_r, dn_s, dn_r,
):
    row, col = lax.axis_index("row"), lax.axis_index("col")
    y, k, z, x = row // NK, row % NK, col // NX, col % NX

    def dev(dy=0, dk=0, dz=0, dx=0):
        return {
            "row": lax.rem(y + dy, NY) * NK + lax.rem(k + dk, NK),
            "col": lax.rem(z + dz, NZ) * NX + lax.rem(x + dx, NX),
        }

    def send(source, target, send_sem, recv_sem, **to):
        copy = pltpu.make_async_remote_copy(
            source, target, send_sem, recv_sem, device_id=dev(**to), device_id_type=MESH
        )
        copy.start()

    def wait(ref, sem):
        pltpu.make_async_copy(ref, ref, sem).wait()

    barrier = pltpu.get_barrier_semaphore()
    for dy, dk, dx in WIDE_PEERS:
        pl.semaphore_signal(barrier, 1, device_id=dev(dy, dk, 0, dx), device_id_type=MESH)
    for dz in Z_PEERS:
        pl.semaphore_signal(barrier, 1, device_id=dev(dz=dz), device_id_type=MESH)

    tf[...] = tgt[...].astype(F32)
    t4[:NJ, :] = tgt[...]
    ls2 = lsm[...] * LOG2E
    lt2 = ltm[...] * LOG2E
    sqy = squared_norms(tgt[...]) * NORM
    aux[0:1, :] = lt2
    aux[1:2, :] = sqy
    acol[...] = to_column(lt2 - sqy)
    pl.semaphore_wait(barrier, len(WIDE_PEERS) + len(Z_PEERS))
    half = pl.ds(pl.multiple_of(k * HALF, HALF), HALF)
    other = pl.ds(pl.multiple_of((1 - k) * HALF, HALF), HALF)
    for dx in X_PEERS:
        send(aux, auxr.at[dx - 1], aux_s, aux_r, dx=dx)
    for dx in X_PEERS:
        send(tf.at[half], trecv.at[dx - 1, half], pf_s, pf_r.at[dx - 1], dx=dx)

    for c in range(NI // 256):
        xt[:, c * 256 : (c + 1) * 256] = nt_dot(tgt[...], src[c * 256 : (c + 1) * 256, :]) * (2 * NORM)

    def f_local(out):
        def tile(t, carry):
            lanes = pl.ds(pl.multiple_of(t * 128, 128), 128)
            for b in range(4):
                rows = slice(b * 128, (b + 1) * 128)
                scores = (xt[rows, lanes] + acol[rows, :]).reshape(16, 8, 128)
                peak = jnp.max(scores, axis=0)
                total = jnp.sum(jnp.exp2(scores - peak[None]), axis=0)
                fparts[b * 8 : (b + 1) * 8, lanes] = peak + log2(total)
            return carry

        lax.fori_loop(0, NI // 128, tile, 0)
        out[...] = merge_rows(fparts[...])

    def f_round(it):
        f_local(lf.at[it, 0])
        for dx in X_PEERS:
            send(lf.at[it, 0], lfx.at[it, dx - 1], fx_s.at[it], fx_r.at[it], dx=dx)
        if it == 0:
            for z2 in range(NZ):
                own[z2 * OWN : (z2 + 1) * OWN, :] = src[pl.ds(pl.multiple_of((z2 * NX + x) * OWN, OWN), OWN), :]
        wait(lfx.at[it], fx_r.at[it])
        lf[it, 1] = merge([lf[it, 0]] + [lfx[it, dx - 1] for dx in X_PEERS])
        for dz in Z_PEERS:
            send(lf.at[it, 1], lfz.at[it, dz - 1], fz_s.at[it], fz_r.at[it], dz=dz)

    def f_end(it, sqx):
        wait(lfz.at[it], fz_r.at[it])
        f2 = sqx - merge([lf[it, 1]] + [lfz[it, dz - 1] for dz in Z_PEERS])
        return ls2 + f2 - sqx

    def g_local(out):
        def group(r, carry):
            rows = pl.ds(pl.multiple_of(r * 8, 8), 8)
            tiles = [
                xt[rows, t * 128 : (t + 1) * 128] + browb[:, t * 128 : (t + 1) * 128] for t in range(NI // 128)
            ]
            peak = functools.reduce(jnp.maximum, tiles)
            total = sum(jnp.exp2(tile - peak) for tile in tiles)
            gparts[rows, :] = peak + log2(total)
            return carry

        lax.fori_loop(0, NJ // 8, group, 0)
        out[...] = merge_rows(gparts[...].T)

    f_round(0)
    sqx = jnp.concatenate(
        [squared_norms(src[c * 256 : (c + 1) * 256, :]) for c in range(NI // 256)], axis=1
    ) * NORM
    brow = f_end(0, sqx)
    browb[...] = jnp.broadcast_to(brow, (8, NI))
    g_local(lg.at[0])
    for n, (dy, dk) in enumerate(ROW_PEERS):
        send(lg.at[0], lgr.at[n], gr_s, gr_r, dy=dy, dk=dk)
    wait(lgr, gr_r)
    g2 = sqy - merge([lg[0]] + [lgr[n] for n in range(len(ROW_PEERS))])
    acol[...] = to_column(lt2 + g2 - sqy)

    f_round(1)
    for dx in X_PEERS:
        wait(trecv.at[dx - 1, half], pf_r.at[dx - 1])
        send(trecv.at[dx - 1, half], trecv.at[dx - 1, half], sib_s, sib_r.at[dx - 1], dk=1)
    brow = f_end(1, sqx)
    browb[...] = jnp.broadcast_to(brow, (8, NI))
    g_local(lg.at[1])
    for n, (dy, dk, dx) in enumerate(WIDE_PEERS):
        send(lg.at[1], lgw.at[n], gw_s, gw_r, dy=dy, dk=dk, dx=dx)

    lcol = to_column(lg[1])
    for b in range(4):
        rows = slice(b * 128, (b + 1) * 128)
        weights = jnp.exp2(xt[rows, :] + brow - lcol[rows, :1]).astype(BF16)
        tn[rows, :] = jnp.dot(weights, src[...], preferred_element_type=F32)
    send(tn.at[other], tsib, ts_s, ts_r, dk=1)

    bcol[...] = to_column(brow)
    for dx in X_PEERS:
        wait(trecv.at[dx - 1, other], sib_r.at[dx - 1])
        t4[dx * NJ : (dx + 1) * NJ, :] = trecv[dx - 1].astype(BF16)
    for dx in range(NX):
        block = slice(dx * NJ, (dx + 1) * NJ)
        x2[:, block] = nt_dot(own[...], t4[block, :]) * (2 * NORM)

    wait(auxr, aux_r)
    wait(lgw, gw_r)
    arow = []
    for b in range(NX):
        parts = [lgw[n] for n, (dy, dk, dx) in enumerate(WIDE_PEERS) if dx == b]
        if b == 0:
            total = merge([lg[1]] + parts)
            arow.append(lt2 + (sqy - total) - sqy)
            shares = [jnp.exp2(lg[1] - total), jnp.exp2(lgw[WIDE_PEERS.index((0, 1, 0))] - total)]
        else:
            mass, norm = auxr[b - 1, 0:1, :], auxr[b - 1, 1:2, :]
            arow.append(mass + (norm - merge(parts)) - norm)
    arow = jnp.concatenate(arow, axis=1)

    wait(tsib, ts_r)
    dn[0] = shares[0]
    dn[1] = shares[1]
    mine, theirs = to_column(dn[0]), to_column(dn[1])
    gparts[...] = mine
    acol[...] = theirs
    tc[...] = tn[half, :] * gparts[half, :1] + tsib[...] * acol[half, :1]
    for dy in Y_PEERS:
        quarter = pl.ds(pl.multiple_of(lax.rem(y + dy, NY) * QUART, QUART), QUART)
        send(tc.at[quarter], ty.at[dy - 1], ty_s, ty_r, dy=dy)

    for z2 in range(NZ):
        rows = slice(z2 * OWN, (z2 + 1) * OWN)
        bias = bcol[pl.ds(pl.multiple_of((z2 * NX + x) * OWN, OWN), OWN), :1]
        plan = jnp.exp2(x2[rows, :] + bias + arow)
        dparts[rows, :] = sum(plan[:, t * 128 : (t + 1) * 128] for t in range(NX * NJ // 128))
        num[z2] = jnp.dot(plan.astype(BF16), t4[...], preferred_element_type=F32)
    dn[2] = jnp.sum(dparts[...].T, axis=0, keepdims=True)

    def block(dz):
        return num.at[lax.rem(z + dz, NZ)]

    def hop(s, c):
        rows = pl.ds(c * 32, 32)
        if s == 0:
            if c == 0:
                send(block(4).at[pl.ds(0, 32)], plus.at[0, 0], plus_s.at[0, 0], plus_r.at[0, 0], dz=1)
            else:
                send(block(4).at[pl.ds(32, 32)], minus.at[0, 1], minus_s.at[0, 1], minus_r.at[0, 1], dz=NZ - 1)
            return
        for way, buf, ssem, rsem, to in (
            (1, plus, plus_s, plus_r, 1),
            (-1, minus, minus_s, minus_r, NZ - 1),
        ):
            mine = block((way * (4 - s)) % NZ).at[rows]
            if s > 1 or (way == 1) == (c == 0):
                wait(buf.at[s - 1, c], rsem.at[s - 1, c])
                mine[...] = mine[...] + buf[s - 1, c]
            send(mine, buf.at[s, c], ssem.at[s, c], rsem.at[s, c], dz=to)

    hop(0, 0)
    hop(0, 1)
    for dz in Z_PEERS:
        send(dn.at[2], dnr.at[dz - 1], dn_s, dn_r, dz=dz)
    hop(1, 0)
    hop(1, 1)
    hop(2, 0)
    hop(2, 1)

    place = pl.ds(pl.multiple_of(k * HALF + y * QUART, QUART), QUART)
    wait(ty, ty_r)
    tout[place, :] = tc[pl.ds(pl.multiple_of(y * QUART, QUART), QUART), :] + ty[0] + ty[1] + ty[2]
    for dy in Y_PEERS:
        send(tout.at[place], tout.at[place], ta_s, ta_r.at[dy - 1], dy=dy)
    send(tout.at[place], tout.at[place], tb_s, tb_r, dk=1)

    hop(3, 0)
    hop(3, 1)
    for dy in (1, 3, 2):
        theirs = pl.ds(pl.multiple_of(k * HALF + lax.rem(y + NY - dy, NY) * QUART, QUART), QUART)
        wait(tout.at[theirs], ta_r.at[dy - 1])
        send(tout.at[theirs], tout.at[theirs], tb_s, tb_r, dk=1)

    wait(dnr, dn_r)
    denom = dn[2]
    for dz in Z_PEERS:
        denom = denom + dnr[dz - 1]
    dparts[...] = to_column(denom)
    inverse = 1.0 / dparts[pl.ds(pl.multiple_of(z * OWN, OWN), OWN), :1]
    for c in range(2):
        rows = slice(c * 32, (c + 1) * 32)
        wait(plus.at[3, c], plus_r.at[3, c])
        wait(minus.at[3, c], minus_r.at[3, c])
        simg[rows, :] = (num[z, rows, :] + plus[3, c] + minus[3, c]) * inverse[rows]
    wait(tout.at[other], tb_r)
    timg[...] = tout[...]

    wait(auxr, aux_s)
    wait(trecv.at[:, half], pf_s)
    wait(trecv.at[:, half], sib_s)
    for it in range(2):
        wait(lfx.at[it], fx_s.at[it])
        wait(lfz.at[it], fz_s.at[it])
    wait(lgr, gr_s)
    wait(lgw, gw_s)
    wait(tsib, ts_s)
    wait(ty, ty_s)
    wait(ty, ta_s)
    wait(tout.at[half], tb_s)
    wait(dnr, dn_s)
    for s in range(4):
        for c in range(2):
            if s > 0 or c == 0:
                wait(plus.at[s, c], plus_s.at[s, c])
            if s > 0 or c == 1:
                wait(minus.at[s, c], minus_s.at[s, c])


def on_device(source, target, log_source_mass, log_target_mass):
    dma, vmem = pltpu.SemaphoreType.DMA, pltpu.VMEM
    scratch = [
        vmem((NJ, NI), F32),
        vmem((NX * OWN * NZ // 4, NX * NJ), F32),
        vmem((NX * NJ, D), BF16),
        vmem((NJ, D), F32),
        vmem((NX - 1, NJ, D), F32),
        vmem((NZ * OWN, D), BF16),
        vmem((32, NI), F32),
        vmem((NJ, 128), F32),
        vmem((NJ, 128), F32),
        vmem((8, NI), F32),
        vmem((NZ, OWN, D), F32),
        vmem((NZ * OWN, 128), F32),
        vmem((2, NJ), F32),
        vmem((NX - 1, 2, NJ), F32),
        vmem((2, 2, 1, NI), F32),
        vmem((2, NX - 1, 1, NI), F32),
        vmem((2, NZ - 1, 1, NI), F32),
        vmem((2, 1, NJ), F32),
        vmem((len(ROW_PEERS), 1, NJ), F32),
        vmem((len(WIDE_PEERS), 1, NJ), F32),
        vmem((NI, 128), F32),
        vmem((NJ, D), F32),
        vmem((HALF, D), F32),
        vmem((HALF, D), F32),
        vmem((NY - 1, QUART, D), F32),
        vmem((NJ, D), F32),
        vmem((4, 2, 32, D), F32),
        vmem((4, 2, 32, D), F32),
        vmem((3, 1, NJ), F32),
        vmem((NZ - 1, 1, NJ), F32),
        dma, dma((3,)), dma, dma((3,)), dma, dma,
        dma((2,)), dma((2,)), dma((2,)), dma((2,)),
        dma, dma, dma, dma,
        dma, dma, dma, dma, dma, dma((3,)), dma, dma,
        dma((4, 2)), dma((4, 2)), dma((4, 2)), dma((4, 2)), dma, dma,
    ]
    return pl.pallas_call(
        kernel,
        out_shape=(jax.ShapeDtypeStruct((OWN, D), F32), jax.ShapeDtypeStruct((NJ, D), F32)),
        in_specs=[pl.BlockSpec(memory_space=vmem)] * 4,
        out_specs=(pl.BlockSpec(memory_space=vmem),) * 2,
        scratch_shapes=scratch,
        compiler_params=pltpu.CompilerParams(
            collective_id=0, has_side_effects=True, vmem_limit_bytes=56 * 2**20
        ),
        cost_estimate=pl.CostEstimate(flops=8 * NI * NJ * D, bytes_accessed=4 * 2**20, transcendentals=7 * NI * NJ),
        name="sinkhorn",
    )(source, target, log_source_mass.reshape(1, NI), log_target_mass.reshape(1, NJ))


def solution(mesh):
    in_specs = (P("row", None), P("col", None), P("row"), P("col"))
    out_specs = (P(("row", "col"), None), P("col", None))
    return jax.shard_map(
        on_device, mesh=mesh, in_specs=in_specs, out_specs=out_specs, check_vma=False
    )
```

time: 622 us -> 93.8 us (0.15)
  blocking collectives: 429 us -> 0 us
  waiting for transfers between devices: 128 us -> 0 us
  Pallas kernels: 0 us -> 89.2 us
  other arithmetic: 30.9 us -> 0 us
  matrix products: 17 us -> 0 us
  between operations: 14.2 us -> 0.64 us
    psum x6 -> x0, blocking collectives: 224 us -> none  [the longest x2 114 us: across_targets(): total = lax.psum(jnp.sum(jnp.exp(scores - peak[:, None]), axis=1), 'col')]
    pmax x4 -> x0, blocking collectives: 205 us -> none  [the longest x2 124 us: across_targets(): peak = lax.pmax(local_peak, 'col')]
    psum x2 -> x0, waiting for transfers between devices: 128 us -> none  [the longest x1 128 us: on_device(): full_numer, full_denom = lax.psum((src_numer, src_denom), 'col')]
    pallas_call x0 -> x1, Pallas kernels: none -> 89.2 us  [on_device(): pl.pallas_call(kernel, out_shape=(jax.ShapeDtypeStruct((OWN, D), F32), ja...]
    dot_general x3 -> x0, matrix products: 17 us -> none  [the longest x1 5.79 us: on_device(): src_numer = jnp.dot(weights, target, preferred_element_type=jnp.float32)]
    reduce_sum x5 -> x0, other arithmetic: 15.5 us -> none  [the longest x2 6.74 us: across_targets(): total = lax.psum(jnp.sum(jnp.exp(scores - peak[:, None]), axis=1), 'col')]
    reduce_max x3 -> x0, other arithmetic: 8.12 us -> none  [the longest x2 5.31 us: across_sources(): local_peak = jnp.max(scores, axis=0)]
  transfers between devices with their start and end apart: 2 -> 0, of which waited for: 1 -> 0; matrix products, arithmetic and copies ran while one was open for 2% -> 0% of each run, Pallas kernels for 0% -> 0%
where the time goes in v1:
time: 93.8 us; the launch traced here: 93.7 us
  Pallas kernels  89.2 us (95%)
  local copies, waits for them, and re-layouts  3.83 us (4%)
    pallas_call x1, Pallas kernels, on_device(): pl.pallas_call(kernel, out_shape=(jax.ShapeDtypeStruct((OWN, D), F32), ja...  89.2 us
    unnamed x2, local copies, waits for them, and re-layouts  3.83 us

profile of v1, /device:TPU:1, one launch (start us, length us, event | category | flops | bytes accessed | tf_op | source)
XLA Modules:
  0.0 93.7 jit_solution(11757415463748010647)
XLA Ops:
  0.6 89.2 %sinkhorn.1 = (f32[64,512]{1,0:T(8,128)}, f32[512,512]{1,0:T(8,128)}) custom-call(bf16[2048,512]{1,0:T(8,128)(2,1)} %src.1, bf16[512,512]{1,0:T(8,128)(2,1)} %tgt.1, f32[1,2048]{1,0:T(1,128)} %bitcast.2, f32[1,512]{1,0:T(1,128)} %bitcast.3), custom_call_target="tpu_custom_call" | custom-call | flops 4294967296 | bytes 4194304 | tf_op jit(solution)/shard_map/sinkhorn/pallas_call | solution.py:350
  89.8 1.6 %copy.8 = f32[64,512]{1,0:T(8,128)} copy(f32[64,512]{1,0:T(8,128)} %get-tuple-element.4) | data formatting | bytes 262144
  91.4 2.3 %copy.9 = f32[512,512]{1,0:T(8,128)} copy(f32[512,512]{1,0:T(8,128)} %get-tuple-element.5) | data formatting | bytes 2097152

commit v2 on v1

--- a/solution.py
+++ b/solution.py
@@ -31,6 +31,11 @@
 ]
 
 
+BARRIER_PEERS = (
+    [(0, 0, dz, 0) for dz in Z_PEERS] + [(dy, dk, 0, 0) for dy, dk in ROW_PEERS] + [(0, 0, 0, dx) for dx in X_PEERS]
+)
+
+
 def log2(x):
     return jnp.log(x) * LOG2E
 
@@ -63,11 +68,12 @@
 
 
 def kernel(
-    src, tgt, lsm, ltm, simg, timg,
-    xt, x2, t4, tf, trecv, own, fparts, gparts, acol, browb, num, dparts,
+    src_in, tgt_in, lsm_in, ltm_in, simg, timg,
+    src, tgt, lsm, ltm, in_sem,
+    xt, x2, t4, tf, trecv, own, fparts, gparts, acol, browb, num, dparts, arowb, brown, weights,
     aux, auxr, lf, lfx, lfz, lg, lgr, lgw, bcol,
     tn, tsib, tc, ty, tout, plus, minus, dn, dnr,
-    pf_s, pf_r, sib_s, sib_r, aux_s, aux_r, fx_s, fx_r, fz_s, fz_r, gr_s, gr_r, gw_s, gw_r,
+    pf_s, pf_r, pfn_s, pfn_r, pff_s, pff_r, gw1_s, gw1_r, sib_s, sib_r, aux_s, aux_r, fx_s, fx_r, fz_s, fz_r, gr_s, gr_r, gw_s, gw_r,
     ts_s, ts_r, ty_s, ty_r, ta_s, ta_r, tb_s, tb_r, plus_s, plus_r, minus_s, minus_r, dn_s, dn_r,
 ):
     row, col = lax.axis_index("row"), lax.axis_index("col")
@@ -89,27 +95,27 @@
         pltpu.make_async_copy(ref, ref, sem).wait()
 
     barrier = pltpu.get_barrier_semaphore()
-    for dy, dk, dx in WIDE_PEERS:
-        pl.semaphore_signal(barrier, 1, device_id=dev(dy, dk, 0, dx), device_id_type=MESH)
-    for dz in Z_PEERS:
-        pl.semaphore_signal(barrier, 1, device_id=dev(dz=dz), device_id_type=MESH)
-
-    tf[...] = tgt[...].astype(F32)
-    t4[:NJ, :] = tgt[...]
+    for peer in BARRIER_PEERS:
+        pl.semaphore_signal(barrier, 1, device_id=dev(*peer), device_id_type=MESH)
+    loads = [
+        pltpu.make_async_copy(ref, held, in_sem.at[n])
+        for n, (ref, held) in enumerate(((tgt_in, tgt), (src_in, src), (ltm_in, ltm), (lsm_in, lsm)))
+    ]
+    for load in loads:
+        load.start()
+    for load in loads:
+        load.wait()
+
     ls2 = lsm[...] * LOG2E
     lt2 = ltm[...] * LOG2E
     sqy = squared_norms(tgt[...]) * NORM
     aux[0:1, :] = lt2
     aux[1:2, :] = sqy
     acol[...] = to_column(lt2 - sqy)
-    pl.semaphore_wait(barrier, len(WIDE_PEERS) + len(Z_PEERS))
     half = pl.ds(pl.multiple_of(k * HALF, HALF), HALF)
     other = pl.ds(pl.multiple_of((1 - k) * HALF, HALF), HALF)
-    for dx in X_PEERS:
-        send(aux, auxr.at[dx - 1], aux_s, aux_r, dx=dx)
-    for dx in X_PEERS:
-        send(tf.at[half], trecv.at[dx - 1, half], pf_s, pf_r.at[dx - 1], dx=dx)
-
+    near = pl.ds(pl.multiple_of(k * HALF, HALF), HALF // 2)
+    far = pl.ds(pl.multiple_of(k * HALF + HALF // 2, HALF // 2), HALF // 2)
     for c in range(NI // 256):
         xt[:, c * 256 : (c + 1) * 256] = nt_dot(tgt[...], src[c * 256 : (c + 1) * 256, :]) * (2 * NORM)
 
@@ -124,16 +130,12 @@
                 fparts[b * 8 : (b + 1) * 8, lanes] = peak + log2(total)
             return carry
 
-        lax.fori_loop(0, NI // 128, tile, 0)
+        lax.fori_loop(0, NI // 128, tile, 0, unroll=8)
         out[...] = merge_rows(fparts[...])
 
     def f_round(it):
-        f_local(lf.at[it, 0])
         for dx in X_PEERS:
             send(lf.at[it, 0], lfx.at[it, dx - 1], fx_s.at[it], fx_r.at[it], dx=dx)
-        if it == 0:
-            for z2 in range(NZ):
-                own[z2 * OWN : (z2 + 1) * OWN, :] = src[pl.ds(pl.multiple_of((z2 * NX + x) * OWN, OWN), OWN), :]
         wait(lfx.at[it], fx_r.at[it])
         lf[it, 1] = merge([lf[it, 0]] + [lfx[it, dx - 1] for dx in X_PEERS])
         for dz in Z_PEERS:
@@ -155,10 +157,20 @@
             gparts[rows, :] = peak + log2(total)
             return carry
 
-        lax.fori_loop(0, NJ // 8, group, 0)
+        lax.fori_loop(0, NJ // 8, group, 0, unroll=16)
         out[...] = merge_rows(gparts[...].T)
 
+    f_local(lf.at[0, 0])
+    tf[...] = tgt[...].astype(F32)
+    t4[:NJ, :] = tgt[...]
+    for z2 in range(NZ):
+        own[z2 * OWN : (z2 + 1) * OWN, :] = src[pl.ds(pl.multiple_of((z2 * NX + x) * OWN, OWN), OWN), :]
+    pl.semaphore_wait(barrier, len(BARRIER_PEERS))
     f_round(0)
+    for dx in X_PEERS:
+        send(aux, auxr.at[dx - 1], aux_s, aux_r, dx=dx)
+    for dx in (1, 3):
+        send(tf.at[half], trecv.at[dx - 1, half], pf_s.at[dx - 1], pf_r.at[dx - 1], dx=dx)
     sqx = jnp.concatenate(
         [squared_norms(src[c * 256 : (c + 1) * 256, :]) for c in range(NI // 256)], axis=1
     ) * NORM
@@ -171,63 +183,94 @@
     g2 = sqy - merge([lg[0]] + [lgr[n] for n in range(len(ROW_PEERS))])
     acol[...] = to_column(lt2 + g2 - sqy)
 
+    f_local(lf.at[1, 0])
     f_round(1)
-    for dx in X_PEERS:
+    for dx in (1, 3):
         wait(trecv.at[dx - 1, half], pf_r.at[dx - 1])
-        send(trecv.at[dx - 1, half], trecv.at[dx - 1, half], sib_s, sib_r.at[dx - 1], dk=1)
+    send(trecv.at[0, near], trecv.at[1, near], pfn_s, pfn_r, dx=1)
+    send(trecv.at[2, far], trecv.at[1, far], pff_s, pff_r, dx=3)
+    for dx in (1, 3):
+        send(trecv.at[dx - 1, half], trecv.at[dx - 1, half], sib_s.at[dx - 1], sib_r.at[dx - 1], dk=1)
     brow = f_end(1, sqx)
     browb[...] = jnp.broadcast_to(brow, (8, NI))
     g_local(lg.at[1])
     for n, (dy, dk, dx) in enumerate(WIDE_PEERS):
-        send(lg.at[1], lgw.at[n], gw_s, gw_r, dy=dy, dk=dk, dx=dx)
+        if (dy, dk, dx) == (0, 1, 0):
+            send(lg.at[1], lgw.at[n], gw1_s, gw1_r, dy=dy, dk=dk, dx=dx)
+        else:
+            send(lg.at[1], lgw.at[n], gw_s, gw_r, dy=dy, dk=dk, dx=dx)
 
     lcol = to_column(lg[1])
     for b in range(4):
         rows = slice(b * 128, (b + 1) * 128)
-        weights = jnp.exp2(xt[rows, :] + brow - lcol[rows, :1]).astype(BF16)
-        tn[rows, :] = jnp.dot(weights, src[...], preferred_element_type=F32)
+        shares = jnp.exp2(xt[rows, :] + brow - lcol[rows, :1]).astype(BF16)
+        tn[rows, :] = jnp.dot(shares, src[...], preferred_element_type=F32)
     send(tn.at[other], tsib, ts_s, ts_r, dk=1)
 
+    def wide_scores(dx):
+        block = slice(dx * NJ, (dx + 1) * NJ)
+        if dx > 0:
+            wait(trecv.at[dx - 1, other], sib_r.at[dx - 1])
+            t4[block, :] = trecv[dx - 1].astype(BF16)
+        x2[:, block] = nt_dot(own[...], t4[block, :]) * (2 * NORM)
+
+    wait(trecv.at[1, near], pfn_r)
+    wait(trecv.at[1, far], pff_r)
+    send(trecv.at[1, half], trecv.at[1, half], sib_s.at[1], sib_r.at[1], dk=1)
     bcol[...] = to_column(brow)
-    for dx in X_PEERS:
-        wait(trecv.at[dx - 1, other], sib_r.at[dx - 1])
-        t4[dx * NJ : (dx + 1) * NJ, :] = trecv[dx - 1].astype(BF16)
-    for dx in range(NX):
-        block = slice(dx * NJ, (dx + 1) * NJ)
-        x2[:, block] = nt_dot(own[...], t4[block, :]) * (2 * NORM)
-
-    wait(auxr, aux_r)
-    wait(lgw, gw_r)
-    arow = []
-    for b in range(NX):
-        parts = [lgw[n] for n, (dy, dk, dx) in enumerate(WIDE_PEERS) if dx == b]
-        if b == 0:
-            total = merge([lg[1]] + parts)
-            arow.append(lt2 + (sqy - total) - sqy)
-            shares = [jnp.exp2(lg[1] - total), jnp.exp2(lgw[WIDE_PEERS.index((0, 1, 0))] - total)]
-        else:
-            mass, norm = auxr[b - 1, 0:1, :], auxr[b - 1, 1:2, :]
-            arow.append(mass + (norm - merge(parts)) - norm)
-    arow = jnp.concatenate(arow, axis=1)
-
+    wide_scores(0)
+    wide_scores(1)
+    wide_scores(3)
+
+    wait(lgw.at[0], gw1_r)
+    sibling = WIDE_PEERS.index((0, 1, 0))
+    pair = merge([lg[1], lgw[sibling]])
+    gparts[...] = to_column(jnp.exp2(lg[1] - pair))
+    acol[...] = to_column(jnp.exp2(lgw[sibling] - pair))
     wait(tsib, ts_r)
-    dn[0] = shares[0]
-    dn[1] = shares[1]
-    mine, theirs = to_column(dn[0]), to_column(dn[1])
-    gparts[...] = mine
-    acol[...] = theirs
     tc[...] = tn[half, :] * gparts[half, :1] + tsib[...] * acol[half, :1]
     for dy in Y_PEERS:
         quarter = pl.ds(pl.multiple_of(lax.rem(y + dy, NY) * QUART, QUART), QUART)
         send(tc.at[quarter], ty.at[dy - 1], ty_s, ty_r, dy=dy)
+    wide_scores(2)
+
+    wait(auxr, aux_r)
+    wait(lgw.at[pl.ds(0, len(WIDE_PEERS) - 1)], gw_r)
+    arow = []
+    for b in range(NX):
+        parts = {dk + NK * dy: lgw[n] for n, (dy, dk, dx) in enumerate(WIDE_PEERS) if dx == b}
+        if b == 0:
+            parts[0] = lg[1]
+            total = merge(list(parts.values()))
+            arow.append(lt2 + (sqy - total) - sqy)
+            for dy in range(NY):
+                dn[dy] = jnp.exp2(merge([parts[NK * dy], parts[NK * dy + 1]]) - total)
+        else:
+            mass, norm = auxr[b - 1, 0:1, :], auxr[b - 1, 1:2, :]
+            arow.append(mass + (norm - merge(list(parts.values()))) - norm)
+    arowb[...] = jnp.broadcast_to(jnp.concatenate(arow, axis=1), (16, NX * NJ))
 
     for z2 in range(NZ):
         rows = slice(z2 * OWN, (z2 + 1) * OWN)
-        bias = bcol[pl.ds(pl.multiple_of((z2 * NX + x) * OWN, OWN), OWN), :1]
-        plan = jnp.exp2(x2[rows, :] + bias + arow)
-        dparts[rows, :] = sum(plan[:, t * 128 : (t + 1) * 128] for t in range(NX * NJ // 128))
-        num[z2] = jnp.dot(plan.astype(BF16), t4[...], preferred_element_type=F32)
-    dn[2] = jnp.sum(dparts[...].T, axis=0, keepdims=True)
+        brown[rows, :] = bcol[pl.ds(pl.multiple_of((z2 * NX + x) * OWN, OWN), OWN), :]
+
+    def plan_rows(r, carry):
+        rows = pl.ds(pl.multiple_of(r * 16, 16), 16)
+        bias = brown[rows, :]
+        denom = None
+        for t in range(NX * NJ // 128):
+            lanes = slice(t * 128, (t + 1) * 128)
+            plan = jnp.exp2(x2[rows, lanes] + bias + arowb[:, lanes])
+            denom = plan if denom is None else denom + plan
+            weights[rows, lanes] = plan.astype(BF16)
+        dparts[rows, :] = denom
+        return carry
+
+    lax.fori_loop(0, NZ * OWN // 16, plan_rows, 0, unroll=4)
+    for b in range(4):
+        sums = jnp.dot(weights[b * 128 : (b + 1) * 128, :], t4[...], preferred_element_type=F32)
+        num[2 * b] = sums[:OWN]
+        num[2 * b + 1] = sums[OWN:]
 
     def block(dz):
         return num.at[lax.rem(z + dz, NZ)]
@@ -252,20 +295,26 @@
 
     hop(0, 0)
     hop(0, 1)
+    dn[NY] = jnp.sum(dparts[...].T, axis=0, keepdims=True)
     for dz in Z_PEERS:
-        send(dn.at[2], dnr.at[dz - 1], dn_s, dn_r, dz=dz)
+        send(dn.at[NY], dnr.at[dz - 1], dn_s, dn_r, dz=dz)
+
+    place = pl.ds(pl.multiple_of(k * HALF + y * QUART, QUART), QUART)
+    rows = pl.ds(pl.multiple_of(y * QUART, QUART), QUART)
+    wait(ty, ty_r)
+    for dy in range(NY):
+        gparts[...] = to_column(dn[dy])
+        part = (tc[rows, :] if dy == 0 else ty[dy - 1]) * gparts[place, :1]
+        whole = part if dy == 0 else whole + part
+    tout[place, :] = whole
+    for dy in Y_PEERS:
+        send(tout.at[place], tout.at[place], ta_s, ta_r.at[dy - 1], dy=dy)
+    send(tout.at[place], tout.at[place], tb_s, tb_r, dk=1)
+
     hop(1, 0)
     hop(1, 1)
     hop(2, 0)
     hop(2, 1)
-
-    place = pl.ds(pl.multiple_of(k * HALF + y * QUART, QUART), QUART)
-    wait(ty, ty_r)
-    tout[place, :] = tc[pl.ds(pl.multiple_of(y * QUART, QUART), QUART), :] + ty[0] + ty[1] + ty[2]
-    for dy in Y_PEERS:
-        send(tout.at[place], tout.at[place], ta_s, ta_r.at[dy - 1], dy=dy)
-    send(tout.at[place], tout.at[place], tb_s, tb_r, dk=1)
-
     hop(3, 0)
     hop(3, 1)
     for dy in (1, 3, 2):
@@ -274,7 +323,7 @@
         send(tout.at[theirs], tout.at[theirs], tb_s, tb_r, dk=1)
 
     wait(dnr, dn_r)
-    denom = dn[2]
+    denom = dn[NY]
     for dz in Z_PEERS:
         denom = denom + dnr[dz - 1]
     dparts[...] = to_column(denom)
@@ -288,13 +337,18 @@
     timg[...] = tout[...]
 
     wait(auxr, aux_s)
-    wait(trecv.at[:, half], pf_s)
-    wait(trecv.at[:, half], sib_s)
+    for dx in (1, 3):
+        wait(trecv.at[dx - 1, half], pf_s.at[dx - 1])
+    wait(trecv.at[1, near], pfn_s)
+    wait(trecv.at[1, far], pff_s)
+    for dx in X_PEERS:
+        wait(trecv.at[dx - 1, half], sib_s.at[dx - 1])
     for it in range(2):
         wait(lfx.at[it], fx_s.at[it])
         wait(lfz.at[it], fz_s.at[it])
     wait(lgr, gr_s)
-    wait(lgw, gw_s)
+    wait(lgw.at[0], gw1_s)
+    wait(lgw.at[pl.ds(0, len(WIDE_PEERS) - 1)], gw_s)
     wait(tsib, ts_s)
     wait(ty, ty_s)
     wait(ty, ta_s)
@@ -308,11 +362,21 @@
                 wait(minus.at[s, c], minus_s.at[s, c])
 
 
+def hand_over(simg, timg, simg_out, timg_out):
+    simg_out[...] = simg[...]
+    timg_out[...] = timg[...]
+
+
 def on_device(source, target, log_source_mass, log_target_mass):
     dma, vmem = pltpu.SemaphoreType.DMA, pltpu.VMEM
     scratch = [
+        vmem((NI, D), BF16),
+        vmem((NJ, D), BF16),
+        vmem((1, NI), F32),
+        vmem((1, NJ), F32),
+        dma((4,)),
         vmem((NJ, NI), F32),
-        vmem((NX * OWN * NZ // 4, NX * NJ), F32),
+        vmem((NZ * OWN, NX * NJ), F32),
         vmem((NX * NJ, D), BF16),
         vmem((NJ, D), F32),
         vmem((NX - 1, NJ, D), F32),
@@ -323,6 +387,9 @@
         vmem((8, NI), F32),
         vmem((NZ, OWN, D), F32),
         vmem((NZ * OWN, 128), F32),
+        vmem((16, NX * NJ), F32),
+        vmem((NZ * OWN, 128), F32),
+        vmem((NZ * OWN, NX * NJ), BF16),
         vmem((2, NJ), F32),
         vmem((NX - 1, 2, NJ), F32),
         vmem((2, 2, 1, NI), F32),
@@ -339,18 +406,19 @@
         vmem((NJ, D), F32),
         vmem((4, 2, 32, D), F32),
         vmem((4, 2, 32, D), F32),
-        vmem((3, 1, NJ), F32),
+        vmem((NY + 1, 1, NJ), F32),
         vmem((NZ - 1, 1, NJ), F32),
-        dma, dma((3,)), dma, dma((3,)), dma, dma,
+        dma((3,)), dma((3,)), dma, dma, dma, dma, dma, dma,
+        dma((3,)), dma((3,)), dma, dma,
         dma((2,)), dma((2,)), dma((2,)), dma((2,)),
         dma, dma, dma, dma,
         dma, dma, dma, dma, dma, dma((3,)), dma, dma,
         dma((4, 2)), dma((4, 2)), dma((4, 2)), dma((4, 2)), dma, dma,
     ]
-    return pl.pallas_call(
+    images = pl.pallas_call(
         kernel,
         out_shape=(jax.ShapeDtypeStruct((OWN, D), F32), jax.ShapeDtypeStruct((NJ, D), F32)),
-        in_specs=[pl.BlockSpec(memory_space=vmem)] * 4,
+        in_specs=[pl.BlockSpec(memory_space=pl.ANY)] * 4,
         out_specs=(pl.BlockSpec(memory_space=vmem),) * 2,
         scratch_shapes=scratch,
         compiler_params=pltpu.CompilerParams(
@@ -359,6 +427,13 @@
         cost_estimate=pl.CostEstimate(flops=8 * NI * NJ * D, bytes_accessed=4 * 2**20, transcendentals=7 * NI * NJ),
         name="sinkhorn",
     )(source, target, log_source_mass.reshape(1, NI), log_target_mass.reshape(1, NJ))
+    return pl.pallas_call(
+        hand_over,
+        out_shape=(jax.ShapeDtypeStruct((OWN, D), F32), jax.ShapeDtypeStruct((NJ, D), F32)),
+        in_specs=[pl.BlockSpec(memory_space=vmem)] * 2,
+        out_specs=(pl.BlockSpec(memory_space=vmem),) * 2,
+        name="hand_over",
+    )(*images)
 
 
 def solution(mesh):

time: 93.8 us -> 62.9 us (0.67)
  Pallas kernels: 89.2 us -> 62.1 us
  local copies, waits for them, and re-layouts: 3.83 us -> 0 us
    pallas_call x1, Pallas kernels: 89.2 us -> 59.8 us  [on_device(): pl.pallas_call(kernel, out_shape=(jax.ShapeDtypeStruct((OWN, D), F32), ja...]
    unnamed x2 -> x0, local copies, waits for them, and re-layouts: 3.83 us -> none
    pallas_call x0 -> x1, Pallas kernels: none -> 2.35 us  [on_device(): pl.pallas_call(hand_over, out_shape=(jax.ShapeDtypeStruct((OWN, D), F32),...]
where the time goes in v2:
time: 62.9 us; the launch traced here: 62.8 us
  Pallas kernels  62.1 us (99%)
  between operations  0.64 us (1%)
    pallas_call x1, Pallas kernels, on_device(): pl.pallas_call(kernel, out_shape=(jax.ShapeDtypeStruct((OWN, D), F32), ja...  59.8 us
    pallas_call x1, Pallas kernels, on_device(): pl.pallas_call(hand_over, out_shape=(jax.ShapeDtypeStruct((OWN, D), F32),...  2.35 us

profile of v2, /device:TPU:1, one launch (start us, length us, event | category | flops | bytes accessed | tf_op | source)
XLA Modules:
  0.0 62.8 jit_solution(12254374049395334328)
XLA Ops:
  0.6 59.8 %sinkhorn.1 = (f32[64,512]{1,0:T(8,128)}, f32[512,512]{1,0:T(8,128)}) custom-call(bf16[2048,512]{1,0:T(8,128)(2,1)} %src_in.1, bf16[512,512]{1,0:T(8,128)(2,1)} %tgt_in.1, f32[1,2048]{1,0:T(1,128)} %bitcast.2, f32[1,512]{1,0:T(1,128)} %bitcast.3), custom_call_target="tpu_custom_call" | custom-call | flops 4294967296 | bytes 4194304 | tf_op jit(solution)/shard_map/sinkhorn/pallas_call | solution.py:418
  60.4 2.4 %hand_over.1 = (f32[64,512]{1,0:T(8,128)}, f32[512,512]{1,0:T(8,128)}) custom-call(f32[64,512]{1,0:T(8,128)} %get-tuple-element.4.simg, f32[512,512]{1,0:T(8,128)} %get-tuple-element.5.timg), custom_call_target="tpu_custom_call" | custom-call | tf_op jit(solution)/shard_map/hand_over/pallas_call | solution.py:430

commit v3 on v2

--- a/solution.py
+++ b/solution.py
@@ -22,6 +22,9 @@
 F32 = jnp.float32
 BF16 = jnp.bfloat16
 
+STEP = 16
+PARTS = OWN // STEP
+ORDER = [4, 3, 5, 2, 6, 1, 7, 0]
 X_PEERS = [1, 2, 3]
 Y_PEERS = [2, 1, 3]
 Z_PEERS = [4, 3, 5, 2, 6, 1, 7]
@@ -54,6 +57,11 @@
     return jnp.broadcast_to(row, (128, row.shape[1])).T
 
 
+def to_columns(rows):
+    rows = rows + [jnp.zeros((128 - len(rows), rows[0].shape[1]), F32)]
+    return jnp.concatenate(rows, axis=0).T
+
+
 def nt_dot(a, b):
     return lax.dot_general(a, b, (((1,), (1,)), ((), ())), preferred_element_type=F32)
 
@@ -68,8 +76,8 @@
 
 
 def kernel(
-    src_in, tgt_in, lsm_in, ltm_in, simg, timg,
-    src, tgt, lsm, ltm, in_sem,
+    src_in, tgt_in, lsm_in, ltm_in, simg_out, timg_out,
+    simg, out_sem,    src, tgt, lsm, ltm, in_sem,
     xt, x2, t4, tf, trecv, own, fparts, gparts, acol, browb, num, dparts, arowb, brown, weights,
     aux, auxr, lf, lfx, lfz, lg, lgr, lgw, bcol,
     tn, tsib, tc, ty, tout, plus, minus, dn, dnr,
@@ -90,6 +98,9 @@
             source, target, send_sem, recv_sem, device_id=dev(**to), device_id_type=MESH
         )
         copy.start()
+
+    def theirs(dz):
+        return pl.ds(pl.multiple_of((lax.rem(z + dz, NZ) * NX + x) * OWN, OWN), OWN)
 
     def wait(ref, sem):
         pltpu.make_async_copy(ref, ref, sem).wait()
@@ -160,11 +171,18 @@
         lax.fori_loop(0, NJ // 8, group, 0, unroll=16)
         out[...] = merge_rows(gparts[...].T)
 
+    def wide_scores(dx):
+        block = slice(dx * NJ, (dx + 1) * NJ)
+        if dx > 0:
+            wait(trecv.at[dx - 1, other], sib_r.at[dx - 1])
+            t4[block, :] = trecv[dx - 1].astype(BF16)
+        x2[:, block] = nt_dot(own[...], t4[block, :]) * (2 * NORM)
+
     f_local(lf.at[0, 0])
     tf[...] = tgt[...].astype(F32)
     t4[:NJ, :] = tgt[...]
-    for z2 in range(NZ):
-        own[z2 * OWN : (z2 + 1) * OWN, :] = src[pl.ds(pl.multiple_of((z2 * NX + x) * OWN, OWN), OWN), :]
+    for n, dz in enumerate(ORDER):
+        own[n * OWN : (n + 1) * OWN, :] = src[theirs(dz), :]
     pl.semaphore_wait(barrier, len(BARRIER_PEERS))
     f_round(0)
     for dx in X_PEERS:
@@ -179,6 +197,7 @@
     g_local(lg.at[0])
     for n, (dy, dk) in enumerate(ROW_PEERS):
         send(lg.at[0], lgr.at[n], gr_s, gr_r, dy=dy, dk=dk)
+    wide_scores(0)
     wait(lgr, gr_r)
     g2 = sqy - merge([lg[0]] + [lgr[n] for n in range(len(ROW_PEERS))])
     acol[...] = to_column(lt2 + g2 - sqy)
@@ -200,38 +219,38 @@
         else:
             send(lg.at[1], lgw.at[n], gw_s, gw_r, dy=dy, dk=dk, dx=dx)
 
-    lcol = to_column(lg[1])
+    gparts[...] = to_column(lg[1])
     for b in range(4):
-        rows = slice(b * 128, (b + 1) * 128)
-        shares = jnp.exp2(xt[rows, :] + brow - lcol[rows, :1]).astype(BF16)
+        start = ((1 - k) * HALF if b < 2 else k * HALF) + b % 2 * 128
+        rows = pl.ds(pl.multiple_of(start, 128), 128)
+        shares = jnp.exp2(xt[rows, :] + brow - gparts[rows, :1]).astype(BF16)
         tn[rows, :] = jnp.dot(shares, src[...], preferred_element_type=F32)
-    send(tn.at[other], tsib, ts_s, ts_r, dk=1)
-
-    def wide_scores(dx):
-        block = slice(dx * NJ, (dx + 1) * NJ)
-        if dx > 0:
-            wait(trecv.at[dx - 1, other], sib_r.at[dx - 1])
-            t4[block, :] = trecv[dx - 1].astype(BF16)
-        x2[:, block] = nt_dot(own[...], t4[block, :]) * (2 * NORM)
+        if b < 2:
+            send(tn.at[rows], tsib.at[pl.ds(b * 128, 128)], ts_s.at[b], ts_r.at[b], dk=1)
 
     wait(trecv.at[1, near], pfn_r)
     wait(trecv.at[1, far], pff_r)
     send(trecv.at[1, half], trecv.at[1, half], sib_s.at[1], sib_r.at[1], dk=1)
     bcol[...] = to_column(brow)
-    wide_scores(0)
     wide_scores(1)
     wide_scores(3)
 
     wait(lgw.at[0], gw1_r)
     sibling = WIDE_PEERS.index((0, 1, 0))
     pair = merge([lg[1], lgw[sibling]])
-    gparts[...] = to_column(jnp.exp2(lg[1] - pair))
-    acol[...] = to_column(jnp.exp2(lgw[sibling] - pair))
-    wait(tsib, ts_r)
-    tc[...] = tn[half, :] * gparts[half, :1] + tsib[...] * acol[half, :1]
-    for dy in Y_PEERS:
-        quarter = pl.ds(pl.multiple_of(lax.rem(y + dy, NY) * QUART, QUART), QUART)
-        send(tc.at[quarter], ty.at[dy - 1], ty_s, ty_r, dy=dy)
+    gparts[...] = to_columns([jnp.exp2(lg[1] - pair), jnp.exp2(lgw[sibling] - pair)])
+    for b in range(2):
+        wait(tsib.at[pl.ds(b * 128, 128)], ts_r.at[b])
+        rows = pl.ds(pl.multiple_of(k * HALF + b * 128, 128), 128)
+        part = slice(b * 128, (b + 1) * 128)
+        tc[part, :] = tn[rows, :] * gparts[rows, :1] + tsib[part, :] * gparts[rows, 1:2]
+    for b in range(2):
+        for dy in Y_PEERS:
+            start = lax.rem(y + dy, NY) * QUART + b * 32
+            send(
+                tc.at[pl.ds(pl.multiple_of(start, 32), 32)], ty.at[dy - 1, pl.ds(b * 32, 32)],
+                ty_s.at[b], ty_r.at[dy - 1, b], dy=dy,
+            )
     wide_scores(2)
 
     wait(auxr, aux_r)
@@ -243,16 +262,15 @@
             parts[0] = lg[1]
             total = merge(list(parts.values()))
             arow.append(lt2 + (sqy - total) - sqy)
-            for dy in range(NY):
-                dn[dy] = jnp.exp2(merge([parts[NK * dy], parts[NK * dy + 1]]) - total)
+            pairs = [merge([parts[NK * dy], parts[NK * dy + 1]]) for dy in range(NY)]
+            gparts[...] = to_columns([jnp.exp2(pair - total) for pair in pairs])
         else:
             mass, norm = auxr[b - 1, 0:1, :], auxr[b - 1, 1:2, :]
             arow.append(mass + (norm - merge(list(parts.values()))) - norm)
     arowb[...] = jnp.broadcast_to(jnp.concatenate(arow, axis=1), (16, NX * NJ))
 
-    for z2 in range(NZ):
-        rows = slice(z2 * OWN, (z2 + 1) * OWN)
-        brown[rows, :] = bcol[pl.ds(pl.multiple_of((z2 * NX + x) * OWN, OWN), OWN), :]
+    for n, dz in enumerate(ORDER):
+        brown[n * OWN : (n + 1) * OWN, :] = bcol[theirs(dz), :]
 
     def plan_rows(r, carry):
         rows = pl.ds(pl.multiple_of(r * 16, 16), 16)
@@ -266,75 +284,97 @@
         dparts[rows, :] = denom
         return carry
 
-    lax.fori_loop(0, NZ * OWN // 16, plan_rows, 0, unroll=4)
-    for b in range(4):
+    def piece(dz, c):
+        return num.at[ORDER.index(dz % NZ), pl.ds(c * STEP, STEP)]
+
+    def hop(s, way, c):
+        buf, ssem, rsem, to = (plus, plus_s, plus_r, 1) if way == 1 else (minus, minus_s, minus_r, NZ - 1)
+        mine = piece(way * (4 - s), c)
+        if s > 1 or s == 1 and (way == 1) == (c < PARTS // 2):
+            wait(buf.at[s - 1, c], rsem.at[s - 1, c])
+            mine[...] = mine[...] + buf[s - 1, c]
+        send(mine, buf.at[s, c], ssem.at[s, c], rsem.at[s, c], dz=to)
+
+    low, high = list(range(PARTS // 2)), list(range(PARTS // 2, PARTS))
+
+    def plan_block(b):
+        lax.fori_loop(b * 8, (b + 1) * 8, plan_rows, 0, unroll=4)
         sums = jnp.dot(weights[b * 128 : (b + 1) * 128, :], t4[...], preferred_element_type=F32)
         num[2 * b] = sums[:OWN]
         num[2 * b + 1] = sums[OWN:]
 
-    def block(dz):
-        return num.at[lax.rem(z + dz, NZ)]
-
-    def hop(s, c):
-        rows = pl.ds(c * 32, 32)
-        if s == 0:
-            if c == 0:
-                send(block(4).at[pl.ds(0, 32)], plus.at[0, 0], plus_s.at[0, 0], plus_r.at[0, 0], dz=1)
-            else:
-                send(block(4).at[pl.ds(32, 32)], minus.at[0, 1], minus_s.at[0, 1], minus_r.at[0, 1], dz=NZ - 1)
-            return
-        for way, buf, ssem, rsem, to in (
-            (1, plus, plus_s, plus_r, 1),
-            (-1, minus, minus_s, minus_r, NZ - 1),
-        ):
-            mine = block((way * (4 - s)) % NZ).at[rows]
-            if s > 1 or (way == 1) == (c == 0):
-                wait(buf.at[s - 1, c], rsem.at[s - 1, c])
-                mine[...] = mine[...] + buf[s - 1, c]
-            send(mine, buf.at[s, c], ssem.at[s, c], rsem.at[s, c], dz=to)
-
-    hop(0, 0)
-    hop(0, 1)
-    dn[NY] = jnp.sum(dparts[...].T, axis=0, keepdims=True)
+    def target_rows(b):
+        place = pl.ds(pl.multiple_of(k * HALF + y * QUART + b * 32, 32), 32)
+        rows = pl.ds(pl.multiple_of(y * QUART + b * 32, 32), 32)
+        shares = gparts[place, :]
+        whole = tc[rows, :] * shares[:, :1]
+        for dy in Y_PEERS:
+            part = ty.at[dy - 1, pl.ds(b * 32, 32)]
+            wait(part, ty_r.at[dy - 1, b])
+            whole = whole + part[...] * shares[:, dy : dy + 1]
+        tout[place, :] = whole
+        for dy in Y_PEERS:
+            send(tout.at[place], tout.at[place], ta_s, ta_r.at[dy - 1, b], dy=dy)
+        send(tout.at[place], tout.at[place], tb_s, tb_r, dk=1)
+
+    def pass_on(dy, b):
+        start = k * HALF + lax.rem(y + NY - dy, NY) * QUART + b * 32
+        place = pl.ds(pl.multiple_of(start, 32), 32)
+        wait(tout.at[place], ta_r.at[dy - 1, b])
+        send(tout.at[place], tout.at[place], tb_s, tb_r, dk=1)
+
+    plan_block(0)
+    for n in range(PARTS // 2):
+        hop(0, 1, low[n])
+        hop(0, -1, high[n])
+    for c in high:
+        hop(1, 1, c)
+    plan_block(1)
+    for c in low:
+        hop(1, -1, c)
+    plan_block(2)
+    plan_block(3)
+    dn[0] = jnp.sum(dparts[...].T, axis=0, keepdims=True)
     for dz in Z_PEERS:
-        send(dn.at[NY], dnr.at[dz - 1], dn_s, dn_r, dz=dz)
-
-    place = pl.ds(pl.multiple_of(k * HALF + y * QUART, QUART), QUART)
-    rows = pl.ds(pl.multiple_of(y * QUART, QUART), QUART)
-    wait(ty, ty_r)
-    for dy in range(NY):
-        gparts[...] = to_column(dn[dy])
-        part = (tc[rows, :] if dy == 0 else ty[dy - 1]) * gparts[place, :1]
-        whole = part if dy == 0 else whole + part
-    tout[place, :] = whole
-    for dy in Y_PEERS:
-        send(tout.at[place], tout.at[place], ta_s, ta_r.at[dy - 1], dy=dy)
-    send(tout.at[place], tout.at[place], tb_s, tb_r, dk=1)
-
-    hop(1, 0)
-    hop(1, 1)
-    hop(2, 0)
-    hop(2, 1)
-    hop(3, 0)
-    hop(3, 1)
-    for dy in (1, 3, 2):
-        theirs = pl.ds(pl.multiple_of(k * HALF + lax.rem(y + NY - dy, NY) * QUART, QUART), QUART)
-        wait(tout.at[theirs], ta_r.at[dy - 1])
-        send(tout.at[theirs], tout.at[theirs], tb_s, tb_r, dk=1)
+        send(dn.at[0], dnr.at[dz - 1], dn_s, dn_r, dz=dz)
+    for n in range(PARTS // 2):
+        hop(1, 1, low[n])
+        hop(1, -1, high[n])
+    target_rows(0)
+    for n in range(PARTS // 2):
+        hop(2, 1, high[n])
+        hop(2, -1, low[n])
+    target_rows(1)
+    for n in range(PARTS // 2):
+        hop(2, 1, low[n])
+        hop(2, -1, high[n])
+    for n in range(PARTS):
+        hop(3, 1, (high + low)[n])
+        hop(3, -1, (low + high)[n])
+    for b in range(2):
+        for dy in (1, 3, 2):
+            pass_on(dy, b)
+    mine = pltpu.make_async_copy(tout.at[half], timg_out.at[half], out_sem.at[0])
+    mine.start()
 
     wait(dnr, dn_r)
-    denom = dn[NY]
+    first = ORDER.index(0) * OWN
+    denom = dn[0, :, first : first + OWN]
     for dz in Z_PEERS:
-        denom = denom + dnr[dz - 1]
-    dparts[...] = to_column(denom)
-    inverse = 1.0 / dparts[pl.ds(pl.multiple_of(z * OWN, OWN), OWN), :1]
-    for c in range(2):
-        rows = slice(c * 32, (c + 1) * 32)
+        first = ORDER.index(dz) * OWN
+        denom = denom + dnr[dz - 1, :, first : first + OWN]
+    inverse = 1.0 / to_column(jnp.concatenate([denom, denom], axis=1))[:OWN]
+    for c in high + low:
+        rows = slice(c * STEP, (c + 1) * STEP)
         wait(plus.at[3, c], plus_r.at[3, c])
         wait(minus.at[3, c], minus_r.at[3, c])
-        simg[rows, :] = (num[z, rows, :] + plus[3, c] + minus[3, c]) * inverse[rows]
+        whole = num[ORDER.index(0), rows, :] + plus[3, c] + minus[3, c]
+        simg[rows, :] = whole * inverse[rows, :1]
+    sources = pltpu.make_async_copy(simg, simg_out, out_sem.at[1])
+    sources.start()
     wait(tout.at[other], tb_r)
-    timg[...] = tout[...]
+    swapped = pltpu.make_async_copy(tout.at[other], timg_out.at[other], out_sem.at[2])
+    swapped.start()
 
     wait(auxr, aux_s)
     for dx in (1, 3):
@@ -349,17 +389,21 @@
     wait(lgr, gr_s)
     wait(lgw.at[0], gw1_s)
     wait(lgw.at[pl.ds(0, len(WIDE_PEERS) - 1)], gw_s)
-    wait(tsib, ts_s)
-    wait(ty, ty_s)
+    for b in range(2):
+        wait(tsib.at[pl.ds(b * 128, 128)], ts_s.at[b])
+        wait(ty.at[:, pl.ds(b * 32, 32)], ty_s.at[b])
     wait(ty, ta_s)
     wait(tout.at[half], tb_s)
     wait(dnr, dn_s)
     for s in range(4):
-        for c in range(2):
-            if s > 0 or c == 0:
+        for c in range(PARTS):
+            if s > 0 or c in low:
                 wait(plus.at[s, c], plus_s.at[s, c])
-            if s > 0 or c == 1:
+            if s > 0 or c in high:
                 wait(minus.at[s, c], minus_s.at[s, c])
+    mine.wait()
+    sources.wait()
+    swapped.wait()
 
 
 def hand_over(simg, timg, simg_out, timg_out):
@@ -370,6 +414,8 @@
 def on_device(source, target, log_source_mass, log_target_mass):
     dma, vmem = pltpu.SemaphoreType.DMA, pltpu.VMEM
     scratch = [
+        vmem((OWN, D), F32),
+        dma((3,)),
         vmem((NI, D), BF16),
         vmem((NJ, D), BF16),
         vmem((1, NI), F32),
@@ -404,22 +450,22 @@
         vmem((HALF, D), F32),
         vmem((NY - 1, QUART, D), F32),
         vmem((NJ, D), F32),
-        vmem((4, 2, 32, D), F32),
-        vmem((4, 2, 32, D), F32),
-        vmem((NY + 1, 1, NJ), F32),
+        vmem((4, PARTS, STEP, D), F32),
+        vmem((4, PARTS, STEP, D), F32),
+        vmem((1, 1, NJ), F32),
         vmem((NZ - 1, 1, NJ), F32),
         dma((3,)), dma((3,)), dma, dma, dma, dma, dma, dma,
         dma((3,)), dma((3,)), dma, dma,
         dma((2,)), dma((2,)), dma((2,)), dma((2,)),
         dma, dma, dma, dma,
-        dma, dma, dma, dma, dma, dma((3,)), dma, dma,
-        dma((4, 2)), dma((4, 2)), dma((4, 2)), dma((4, 2)), dma, dma,
+        dma((2,)), dma((2,)), dma((2,)), dma((3, 2)), dma, dma((3, 2)), dma, dma,
+        dma((4, PARTS)), dma((4, PARTS)), dma((4, PARTS)), dma((4, PARTS)), dma, dma,
     ]
     images = pl.pallas_call(
         kernel,
         out_shape=(jax.ShapeDtypeStruct((OWN, D), F32), jax.ShapeDtypeStruct((NJ, D), F32)),
         in_specs=[pl.BlockSpec(memory_space=pl.ANY)] * 4,
-        out_specs=(pl.BlockSpec(memory_space=vmem),) * 2,
+        out_specs=(pl.BlockSpec(memory_space=pl.ANY),) * 2,
         scratch_shapes=scratch,
         compiler_params=pltpu.CompilerParams(
             collective_id=0, has_side_effects=True, vmem_limit_bytes=56 * 2**20

time: 62.9 us -> 59.2 us (0.941)
  Pallas kernels: 62.1 us -> 58.4 us
    pallas_call x1, Pallas kernels: 59.8 us -> 56.1 us  [on_device(): pl.pallas_call(kernel, out_shape=(jax.ShapeDtypeStruct((OWN, D), F32), ja...]
where the time goes in v3:
time: 59.2 us; the launch traced here: 59.1 us
  Pallas kernels  58.4 us (99%)
  between operations  0.64 us (1%)
    pallas_call x1, Pallas kernels, on_device(): pl.pallas_call(kernel, out_shape=(jax.ShapeDtypeStruct((OWN, D), F32), ja...  56.1 us
    pallas_call x1, Pallas kernels, on_device(): pl.pallas_call(hand_over, out_shape=(jax.ShapeDtypeStruct((OWN, D), F32),...  2.35 us

profile of v3, /device:TPU:1, one launch (start us, length us, event | category | flops | bytes accessed | tf_op | source)
XLA Modules:
  0.0 59.1 jit_solution(14610000947276165514)
XLA Ops:
  0.6 56.1 %sinkhorn.1 = (f32[64,512]{1,0:T(8,128)}, f32[512,512]{1,0:T(8,128)}) custom-call(bf16[2048,512]{1,0:T(8,128)(2,1)} %src_in.1, bf16[512,512]{1,0:T(8,128)(2,1)} %tgt_in.1, f32[1,2048]{1,0:T(1,128)} %bitcast.2, f32[1,512]{1,0:T(1,128)} %bitcast.3), custom_call_target="tpu_custom_call" | custom-call | flops 4294967296 | bytes 4194304 | tf_op jit(solution)/shard_map/sinkhorn/pallas_call | solution.py:464
  56.7 2.4 %hand_over.1 = (f32[64,512]{1,0:T(8,128)}, f32[512,512]{1,0:T(8,128)}) custom-call(f32[64,512]{1,0:T(8,128)} %get-tuple-element.4.simg, f32[512,512]{1,0:T(8,128)} %get-tuple-element.5.timg), custom_call_target="tpu_custom_call" | custom-call | tf_op jit(solution)/shard_map/hand_over/pallas_call | solution.py:476

commit v4 on v3

--- a/solution.py
+++ b/solution.py
@@ -110,11 +110,16 @@
         pl.semaphore_signal(barrier, 1, device_id=dev(*peer), device_id_type=MESH)
     loads = [
         pltpu.make_async_copy(ref, held, in_sem.at[n])
-        for n, (ref, held) in enumerate(((tgt_in, tgt), (src_in, src), (ltm_in, ltm), (lsm_in, lsm)))
+        for n, (ref, held) in enumerate(((tgt_in, tgt), (ltm_in, ltm), (lsm_in, lsm)))
+    ] + [
+        pltpu.make_async_copy(
+            src_in.at[pl.ds(c * 512, 512)], src.at[pl.ds(c * 512, 512)], in_sem.at[3 + c]
+        )
+        for c in range(4)
     ]
     for load in loads:
         load.start()
-    for load in loads:
+    for load in loads[:3]:
         load.wait()
 
     ls2 = lsm[...] * LOG2E
@@ -127,26 +132,28 @@
     other = pl.ds(pl.multiple_of((1 - k) * HALF, HALF), HALF)
     near = pl.ds(pl.multiple_of(k * HALF, HALF), HALF // 2)
     far = pl.ds(pl.multiple_of(k * HALF + HALF // 2, HALF // 2), HALF // 2)
-    for c in range(NI // 256):
-        xt[:, c * 256 : (c + 1) * 256] = nt_dot(tgt[...], src[c * 256 : (c + 1) * 256, :]) * (2 * NORM)
+    def f_tile(t):
+        lanes = slice(t * 128, (t + 1) * 128)
+        for b in range(4):
+            rows = slice(b * 128, (b + 1) * 128)
+            scores = (xt[rows, lanes] + acol[rows, :]).reshape(16, 8, 128)
+            peak = jnp.max(scores, axis=0)
+            total = jnp.sum(jnp.exp2(scores - peak[None]), axis=0)
+            fparts[b * 8 : (b + 1) * 8, lanes] = peak + log2(total)
 
     def f_local(out):
-        def tile(t, carry):
-            lanes = pl.ds(pl.multiple_of(t * 128, 128), 128)
-            for b in range(4):
-                rows = slice(b * 128, (b + 1) * 128)
-                scores = (xt[rows, lanes] + acol[rows, :]).reshape(16, 8, 128)
-                peak = jnp.max(scores, axis=0)
-                total = jnp.sum(jnp.exp2(scores - peak[None]), axis=0)
-                fparts[b * 8 : (b + 1) * 8, lanes] = peak + log2(total)
-            return carry
-
-        lax.fori_loop(0, NI // 128, tile, 0, unroll=8)
+        for t in range(NI // 128):
+            f_tile(t)
         out[...] = merge_rows(fparts[...])
 
     def f_round(it):
         for dx in X_PEERS:
             send(lf.at[it, 0], lfx.at[it, dx - 1], fx_s.at[it], fx_r.at[it], dx=dx)
+        if it == 0:
+            tf[...] = tgt[...].astype(F32)
+            t4[:NJ, :] = tgt[...]
+            for n, dz in enumerate(ORDER):
+                own[n * OWN : (n + 1) * OWN, :] = src[theirs(dz), :]
         wait(lfx.at[it], fx_r.at[it])
         lf[it, 1] = merge([lf[it, 0]] + [lfx[it, dx - 1] for dx in X_PEERS])
         for dz in Z_PEERS:
@@ -168,7 +175,7 @@
             gparts[rows, :] = peak + log2(total)
             return carry
 
-        lax.fori_loop(0, NJ // 8, group, 0, unroll=16)
+        lax.fori_loop(0, NJ // 8, group, 0, unroll=64)
         out[...] = merge_rows(gparts[...].T)
 
     def wide_scores(dx):
@@ -178,11 +185,16 @@
             t4[block, :] = trecv[dx - 1].astype(BF16)
         x2[:, block] = nt_dot(own[...], t4[block, :]) * (2 * NORM)
 
-    f_local(lf.at[0, 0])
-    tf[...] = tgt[...].astype(F32)
-    t4[:NJ, :] = tgt[...]
-    for n, dz in enumerate(ORDER):
-        own[n * OWN : (n + 1) * OWN, :] = src[theirs(dz), :]
+    for c in range(NI // 256):
+        if c % 2 == 0:
+            loads[3 + c // 2].wait()
+        xt[:, c * 256 : (c + 1) * 256] = nt_dot(tgt[...], src[c * 256 : (c + 1) * 256, :]) * (2 * NORM)
+        if c > 0:
+            f_tile(2 * c - 2)
+            f_tile(2 * c - 1)
+    f_tile(NI // 128 - 2)
+    f_tile(NI // 128 - 1)
+    lf[0, 0] = merge_rows(fparts[...])
     pl.semaphore_wait(barrier, len(BARRIER_PEERS))
     f_round(0)
     for dx in X_PEERS:
@@ -231,10 +243,6 @@
     wait(trecv.at[1, near], pfn_r)
     wait(trecv.at[1, far], pff_r)
     send(trecv.at[1, half], trecv.at[1, half], sib_s.at[1], sib_r.at[1], dk=1)
-    bcol[...] = to_column(brow)
-    wide_scores(1)
-    wide_scores(3)
-
     wait(lgw.at[0], gw1_r)
     sibling = WIDE_PEERS.index((0, 1, 0))
     pair = merge([lg[1], lgw[sibling]])
@@ -251,6 +259,12 @@
                 tc.at[pl.ds(pl.multiple_of(start, 32), 32)], ty.at[dy - 1, pl.ds(b * 32, 32)],
                 ty_s.at[b], ty_r.at[dy - 1, b], dy=dy,
             )
+    bcol[...] = to_column(brow)
+    for n, dz in enumerate(ORDER):
+        brown[n * OWN : (n + 1) * OWN, :] = bcol[theirs(dz), :]
+    wide_scores(1)
+    wide_scores(3)
+
     wide_scores(2)
 
     wait(auxr, aux_r)
@@ -268,9 +282,6 @@
             mass, norm = auxr[b - 1, 0:1, :], auxr[b - 1, 1:2, :]
             arow.append(mass + (norm - merge(list(parts.values()))) - norm)
     arowb[...] = jnp.broadcast_to(jnp.concatenate(arow, axis=1), (16, NX * NJ))
-
-    for n, dz in enumerate(ORDER):
-        brown[n * OWN : (n + 1) * OWN, :] = bcol[theirs(dz), :]
 
     def plan_rows(r, carry):
         rows = pl.ds(pl.multiple_of(r * 16, 16), 16)
@@ -406,9 +417,21 @@
     swapped.wait()
 
 
-def hand_over(simg, timg, simg_out, timg_out):
-    simg_out[...] = simg[...]
-    timg_out[...] = timg[...]
+def hand_over(simg, timg, simg_out, timg_out, rows, parts, sem):
+    count = parts.shape[0]
+    size = NJ // count
+    pairs = [(simg, rows, simg_out)] + [
+        (timg.at[pl.ds(n * size, size)], parts.at[n], timg_out.at[pl.ds(n * size, size)]) for n in range(count)
+    ]
+    loads = [pltpu.make_async_copy(a, b, sem.at[0, n]) for n, (a, b, _) in enumerate(pairs)]
+    stores = [pltpu.make_async_copy(b, c, sem.at[1, n]) for n, (_, b, c) in enumerate(pairs)]
+    for load in loads:
+        load.start()
+    for load, store in zip(loads, stores):
+        load.wait()
+        store.start()
+    for store in stores:
+        store.wait()
 
 
 def on_device(source, target, log_source_mass, log_target_mass):
@@ -420,7 +443,7 @@
         vmem((NJ, D), BF16),
         vmem((1, NI), F32),
         vmem((1, NJ), F32),
-        dma((4,)),
+        dma((7,)),
         vmem((NJ, NI), F32),
         vmem((NZ * OWN, NX * NJ), F32),
         vmem((NX * NJ, D), BF16),
@@ -476,8 +499,9 @@
     return pl.pallas_call(
         hand_over,
         out_shape=(jax.ShapeDtypeStruct((OWN, D), F32), jax.ShapeDtypeStruct((NJ, D), F32)),
-        in_specs=[pl.BlockSpec(memory_space=vmem)] * 2,
-        out_specs=(pl.BlockSpec(memory_space=vmem),) * 2,
+        in_specs=[pl.BlockSpec(memory_space=pl.ANY)] * 2,
+        out_specs=(pl.BlockSpec(memory_space=pl.ANY),) * 2,
+        scratch_shapes=[vmem((OWN, D), F32), vmem((4, NJ // 4, D), F32), dma((2, 4+1))],
         name="hand_over",
     )(*images)
 

time: 59.2 us -> 58.2 us (0.983)
  Pallas kernels: 58.4 us -> 57.3 us
    pallas_call x1, Pallas kernels: 56.1 us -> 55.2 us  [on_device(): pl.pallas_call(kernel, out_shape=(jax.ShapeDtypeStruct((OWN, D), F32), ja...]
where the time goes in v4:
time: 58.2 us; the launch traced here: 58.1 us
  Pallas kernels  57.3 us (98%)
  between operations  0.8 us (1%)
    pallas_call x1, Pallas kernels, on_device(): pl.pallas_call(kernel, out_shape=(jax.ShapeDtypeStruct((OWN, D), F32), ja...  55.2 us
    pallas_call x1, Pallas kernels, on_device(): pl.pallas_call(hand_over, out_shape=(jax.ShapeDtypeStruct((OWN, D), F32),...  2.07 us

profile of v4, /device:TPU:1, one launch (start us, length us, event | category | flops | bytes accessed | tf_op | source)
XLA Modules:
  0.0 58.1 jit_solution(6479473606628509253)
XLA Ops:
  0.6 55.2 %sinkhorn.1 = (f32[64,512]{1,0:T(8,128)}, f32[512,512]{1,0:T(8,128)}) custom-call(bf16[2048,512]{1,0:T(8,128)(2,1)} %src_in.1, bf16[512,512]{1,0:T(8,128)(2,1)} %tgt_in.1, f32[1,2048]{1,0:T(1,128)} %bitcast.2, f32[1,512]{1,0:T(1,128)} %bitcast.3), custom_call_target="tpu_custom_call" | custom-call | flops 4294967296 | bytes 4194304 | tf_op jit(solution)/shard_map/sinkhorn/pallas_call | solution.py:487
  55.9 2.1 %hand_over.1 = (f32[64,512]{1,0:T(8,128)}, f32[512,512]{1,0:T(8,128)}) custom-call(f32[64,512]{1,0:T(8,128)} %get-tuple-element.4.simg, f32[512,512]{1,0:T(8,128)} %get-tuple-element.5.timg), custom_call_target="tpu_custom_call" | custom-call | tf_op jit(solution)/shard_map/hand_over/pallas_call | solution.py:499

commit v5 on v4

--- a/solution.py
+++ b/solution.py
@@ -222,6 +222,7 @@
     send(trecv.at[2, far], trecv.at[1, far], pff_s, pff_r, dx=3)
     for dx in (1, 3):
         send(trecv.at[dx - 1, half], trecv.at[dx - 1, half], sib_s.at[dx - 1], sib_r.at[dx - 1], dk=1)
+    wide_scores(1)
     brow = f_end(1, sqx)
     browb[...] = jnp.broadcast_to(brow, (8, NI))
     g_local(lg.at[1])
@@ -229,7 +230,7 @@
         if (dy, dk, dx) == (0, 1, 0):
             send(lg.at[1], lgw.at[n], gw1_s, gw1_r, dy=dy, dk=dk, dx=dx)
         else:
-            send(lg.at[1], lgw.at[n], gw_s, gw_r, dy=dy, dk=dk, dx=dx)
+            send(lg.at[1], lgw.at[n], gw_s, gw_r.at[dx], dy=dy, dk=dk, dx=dx)
 
     gparts[...] = to_column(lg[1])
     for b in range(4):
@@ -243,6 +244,9 @@
     wait(trecv.at[1, near], pfn_r)
     wait(trecv.at[1, far], pff_r)
     send(trecv.at[1, half], trecv.at[1, half], sib_s.at[1], sib_r.at[1], dk=1)
+    bcol[...] = to_column(brow)
+    for n, dz in enumerate(ORDER):
+        brown[n * OWN : (n + 1) * OWN, :] = bcol[theirs(dz), :]
     wait(lgw.at[0], gw1_r)
     sibling = WIDE_PEERS.index((0, 1, 0))
     pair = merge([lg[1], lgw[sibling]])
@@ -259,29 +263,25 @@
                 tc.at[pl.ds(pl.multiple_of(start, 32), 32)], ty.at[dy - 1, pl.ds(b * 32, 32)],
                 ty_s.at[b], ty_r.at[dy - 1, b], dy=dy,
             )
-    bcol[...] = to_column(brow)
-    for n, dz in enumerate(ORDER):
-        brown[n * OWN : (n + 1) * OWN, :] = bcol[theirs(dz), :]
-    wide_scores(1)
+
     wide_scores(3)
-
     wide_scores(2)
 
     wait(auxr, aux_r)
-    wait(lgw.at[pl.ds(0, len(WIDE_PEERS) - 1)], gw_r)
-    arow = []
-    for b in range(NX):
+    arow = {}
+    for b in (0, 1, 3, 2):
+        wait(lgw.at[pl.ds(0, NY * NK - (2 if b == 0 else 0))], gw_r.at[b])
         parts = {dk + NK * dy: lgw[n] for n, (dy, dk, dx) in enumerate(WIDE_PEERS) if dx == b}
         if b == 0:
             parts[0] = lg[1]
             total = merge(list(parts.values()))
-            arow.append(lt2 + (sqy - total) - sqy)
+            arow[b] = lt2 + (sqy - total) - sqy
             pairs = [merge([parts[NK * dy], parts[NK * dy + 1]]) for dy in range(NY)]
             gparts[...] = to_columns([jnp.exp2(pair - total) for pair in pairs])
         else:
             mass, norm = auxr[b - 1, 0:1, :], auxr[b - 1, 1:2, :]
-            arow.append(mass + (norm - merge(list(parts.values()))) - norm)
-    arowb[...] = jnp.broadcast_to(jnp.concatenate(arow, axis=1), (16, NX * NJ))
+            arow[b] = mass + (norm - merge(list(parts.values()))) - norm
+        arowb[:, b * NJ : (b + 1) * NJ] = jnp.broadcast_to(arow[b], (16, NJ))
 
     def plan_rows(r, carry):
         rows = pl.ds(pl.multiple_of(r * 16, 16), 16)
@@ -333,6 +333,13 @@
         place = pl.ds(pl.multiple_of(start, 32), 32)
         wait(tout.at[place], ta_r.at[dy - 1, b])
         send(tout.at[place], tout.at[place], tb_s, tb_r, dk=1)
+
+    def left(s):
+        for c in range(PARTS):
+            if s > 0 or c in low:
+                wait(plus.at[s, c], plus_s.at[s, c])
+            if s > 0 or c in high:
+                wait(minus.at[s, c], minus_s.at[s, c])
 
     plan_block(0)
     for n in range(PARTS // 2):
@@ -352,6 +359,22 @@
         hop(1, 1, low[n])
         hop(1, -1, high[n])
     target_rows(0)
+    wait(auxr, aux_s)
+    for dx in (1, 3):
+        wait(trecv.at[dx - 1, half], pf_s.at[dx - 1])
+    wait(trecv.at[1, near], pfn_s)
+    wait(trecv.at[1, far], pff_s)
+    for dx in X_PEERS:
+        wait(trecv.at[dx - 1, half], sib_s.at[dx - 1])
+    for it in range(2):
+        wait(lfx.at[it], fx_s.at[it])
+        wait(lfz.at[it], fz_s.at[it])
+    wait(lgr, gr_s)
+    wait(lgw.at[0], gw1_s)
+    wait(lgw.at[pl.ds(0, len(WIDE_PEERS) - 1)], gw_s)
+    for b in range(2):
+        wait(tsib.at[pl.ds(b * 128, 128)], ts_s.at[b])
+        wait(ty.at[:, pl.ds(b * 32, 32)], ty_s.at[b])
     for n in range(PARTS // 2):
         hop(2, 1, high[n])
         hop(2, -1, low[n])
@@ -359,12 +382,15 @@
     for n in range(PARTS // 2):
         hop(2, 1, low[n])
         hop(2, -1, high[n])
+    left(0)
+    left(1)
     for n in range(PARTS):
         hop(3, 1, (high + low)[n])
         hop(3, -1, (low + high)[n])
     for b in range(2):
         for dy in (1, 3, 2):
             pass_on(dy, b)
+    left(2)
     mine = pltpu.make_async_copy(tout.at[half], timg_out.at[half], out_sem.at[0])
     mine.start()
 
@@ -387,31 +413,10 @@
     swapped = pltpu.make_async_copy(tout.at[other], timg_out.at[other], out_sem.at[2])
     swapped.start()
 
-    wait(auxr, aux_s)
-    for dx in (1, 3):
-        wait(trecv.at[dx - 1, half], pf_s.at[dx - 1])
-    wait(trecv.at[1, near], pfn_s)
-    wait(trecv.at[1, far], pff_s)
-    for dx in X_PEERS:
-        wait(trecv.at[dx - 1, half], sib_s.at[dx - 1])
-    for it in range(2):
-        wait(lfx.at[it], fx_s.at[it])
-        wait(lfz.at[it], fz_s.at[it])
-    wait(lgr, gr_s)
-    wait(lgw.at[0], gw1_s)
-    wait(lgw.at[pl.ds(0, len(WIDE_PEERS) - 1)], gw_s)
-    for b in range(2):
-        wait(tsib.at[pl.ds(b * 128, 128)], ts_s.at[b])
-        wait(ty.at[:, pl.ds(b * 32, 32)], ty_s.at[b])
     wait(ty, ta_s)
     wait(tout.at[half], tb_s)
     wait(dnr, dn_s)
-    for s in range(4):
-        for c in range(PARTS):
-            if s > 0 or c in low:
-                wait(plus.at[s, c], plus_s.at[s, c])
-            if s > 0 or c in high:
-                wait(minus.at[s, c], minus_s.at[s, c])
+    left(3)
     mine.wait()
     sources.wait()
     swapped.wait()
@@ -480,7 +485,7 @@
         dma((3,)), dma((3,)), dma, dma, dma, dma, dma, dma,
         dma((3,)), dma((3,)), dma, dma,
         dma((2,)), dma((2,)), dma((2,)), dma((2,)),
-        dma, dma, dma, dma,
+        dma, dma, dma, dma((NX,)),
         dma((2,)), dma((2,)), dma((2,)), dma((3, 2)), dma, dma((3, 2)), dma, dma,
         dma((4, PARTS)), dma((4, PARTS)), dma((4, PARTS)), dma((4, PARTS)), dma, dma,
     ]

time: 58.2 us -> 58 us (level)
  no operation moved by 1% of the time
where the time goes in v5:
time: 58 us; the launch traced here: 57.9 us
  Pallas kernels  57.1 us (98%)
  between operations  0.8 us (1%)
    pallas_call x1, Pallas kernels, on_device(): pl.pallas_call(kernel, out_shape=(jax.ShapeDtypeStruct((OWN, D), F32), ja...  55 us
    pallas_call x1, Pallas kernels, on_device(): pl.pallas_call(hand_over, out_shape=(jax.ShapeDtypeStruct((OWN, D), F32),...  2.07 us

profile of v5, /device:TPU:1, one launch (start us, length us, event | category | flops | bytes accessed | tf_op | source)
XLA Modules:
  0.0 57.9 jit_solution(7507215167146062933)
XLA Ops:
  0.6 55.0 %sinkhorn.1 = (f32[64,512]{1,0:T(8,128)}, f32[512,512]{1,0:T(8,128)}) custom-call(bf16[2048,512]{1,0:T(8,128)(2,1)} %src_in.1, bf16[512,512]{1,0:T(8,128)(2,1)} %tgt_in.1, f32[1,2048]{1,0:T(1,128)} %bitcast.2, f32[1,512]{1,0:T(1,128)} %bitcast.3), custom_call_target="tpu_custom_call" | custom-call | flops 4294967296 | bytes 4194304 | tf_op jit(solution)/shard_map/sinkhorn/pallas_call | solution.py:492
  55.7 2.1 %hand_over.1 = (f32[64,512]{1,0:T(8,128)}, f32[512,512]{1,0:T(8,128)}) custom-call(f32[64,512]{1,0:T(8,128)} %get-tuple-element.4.simg, f32[512,512]{1,0:T(8,128)} %get-tuple-element.5.timg), custom_call_target="tpu_custom_call" | custom-call | tf_op jit(solution)/shard_map/hand_over/pallas_call | solution.py:504

commit v6 on v5

--- a/solution.py
+++ b/solution.py
@@ -359,6 +359,7 @@
         hop(1, 1, low[n])
         hop(1, -1, high[n])
     target_rows(0)
+    target_rows(1)
     wait(auxr, aux_s)
     for dx in (1, 3):
         wait(trecv.at[dx - 1, half], pf_s.at[dx - 1])
@@ -378,7 +379,6 @@
     for n in range(PARTS // 2):
         hop(2, 1, high[n])
         hop(2, -1, low[n])
-    target_rows(1)
     for n in range(PARTS // 2):
         hop(2, 1, low[n])
         hop(2, -1, high[n])

time: 58 us -> 58 us (level)
  no operation moved by 1% of the time
where the time goes in v6:
time: 58 us; the launch traced here: 57.9 us
  Pallas kernels  57.1 us (98%)
  between operations  0.8 us (1%)
    pallas_call x1, Pallas kernels, on_device(): pl.pallas_call(kernel, out_shape=(jax.ShapeDtypeStruct((OWN, D), F32), ja...  55 us
    pallas_call x1, Pallas kernels, on_device(): pl.pallas_call(hand_over, out_shape=(jax.ShapeDtypeStruct((OWN, D), F32),...  2.07 us

profile of v6, /device:TPU:1, one launch (start us, length us, event | category | flops | bytes accessed | tf_op | source)
XLA Modules:
  0.0 57.9 jit_solution(13058017450140072512)
XLA Ops:
  0.6 55.0 %sinkhorn.1 = (f32[64,512]{1,0:T(8,128)}, f32[512,512]{1,0:T(8,128)}) custom-call(bf16[2048,512]{1,0:T(8,128)(2,1)} %src_in.1, bf16[512,512]{1,0:T(8,128)(2,1)} %tgt_in.1, f32[1,2048]{1,0:T(1,128)} %bitcast.2, f32[1,512]{1,0:T(1,128)} %bitcast.3), custom_call_target="tpu_custom_call" | custom-call | flops 4294967296 | bytes 4194304 | tf_op jit(solution)/shard_map/sinkhorn/pallas_call | solution.py:492
  55.7 2.1 %hand_over.1 = (f32[64,512]{1,0:T(8,128)}, f32[512,512]{1,0:T(8,128)}) custom-call(f32[64,512]{1,0:T(8,128)} %get-tuple-element.4.simg, f32[512,512]{1,0:T(8,128)} %get-tuple-element.5.timg), custom_call_target="tpu_custom_call" | custom-call | tf_op jit(solution)/shard_map/hand_over/pallas_call | solution.py:504
